TPU v7x, 128 devices: a whole 4x4x4 slice. The times are simulated.
128 devices in a mesh: mem: 16 (over x, z_lo, core), lev: 8 (over y, z_hi).
Axes of the slice: x: 4, y: 4, z: 4 (z_hi: 2, z_lo: 2; z = z_hi * 2 + z_lo), core: 2. Of those that a mesh axis runs over, the one named last changes fastest.
Arguments:
- control_vec: float32 [256, 64, 8192], P('mem', 'lev'), may hold values from -6 to 6
- ens_perturb: bfloat16 [256, 3, 64, 8192], P(None, None, 'lev', 'mem'), may hold values from -6 to 6
- loc_blocks: bfloat16 [64, 9, 128, 128], replicated, may hold values from -0.1875 to 0.1875
- tile_index: int32 [64, 9], replicated, may hold values from 0 to 63, all different within a row
- obs_weight: bfloat16 [3, 64, 256], P(None, 'lev'), may hold values from -0.4375 to 0.4375
- channel_level_mask: int32 [64, 256], P('lev'), may hold values 0 or 1
- obs_precision: float32 [256, 8192], P(None, 'mem'), may hold values from 2 to 64
Outputs:
- hess_vec: float32 [256, 64, 8192], P('mem', 'lev')
Inputs may be any that keep to these rules, and one draw needn't show every extreme that they name: `tile_index`: each row names 9 different tiles; every tile is named by some row.
All inputs are finite; a program needn't handle non-finite values. No bound on the sum of `channel_level_mask` on one device may be relied on, other than what follows from the above.
Results may differ from a plain program's by a relative error of at most 0.012.
Values may be sent and summed in bfloat16 or wider, within the bound.
A program may use at most 192 MiB of HBM per device.

v0:
```python
import math
import jax
import jax.numpy as jnp
from jax import lax
from jax.sharding import PartitionSpec as P


def observe_adjoint(analysis_increment, operator, obs_precision):
    channels = operator.shape[2]
    share = channels // lax.axis_size("lev")
    operator_partial = operator
    local_similarity = lax.psum_scatter(
        jnp.einsum(
            "bws,bwn->sn", operator_partial, analysis_increment, preferred_element_type=jnp.float32
        ),
        "lev",
        scatter_dimension=0,
        tiled=True,
    )
    precision_rows = lax.dynamic_slice_in_dim(
        obs_precision, lax.axis_index("lev") * share, share, 0
    )
    weighted = (precision_rows * local_similarity).astype(jnp.bfloat16)
    operator_partial = operator
    gradient = jnp.einsum(
        "nhs,sb->nhb",
        operator_partial,
        lax.all_gather(weighted, "lev", axis=0, tiled=True),
        preferred_element_type=jnp.float32,
    )
    return gradient.astype(jnp.bfloat16)


def body(
    control_vec, ens_perturb, loc_blocks, tile_index, obs_weight, channel_level_mask, obs_precision
):
    mem_rows, lev_rows, points = control_vec.shape
    tile_len = loc_blocks.shape[2]
    tile_count = points // tile_len
    neighbours = tile_index.shape[1]
    row_total = mem_rows * lev_rows
    control_low = control_vec.astype(jnp.bfloat16).reshape(row_total, tile_count, tile_len)
    blocks = jnp.take(control_low, tile_index, axis=1)
    localized = jnp.einsum("rtkj,tkji->rti", blocks, loc_blocks, preferred_element_type=jnp.float32)
    localized = localized.astype(jnp.bfloat16).reshape(mem_rows, lev_rows, points)
    members = ens_perturb.shape[0]
    ens_scale = 1.0 / math.sqrt(members - 1)
    operator = obs_weight * channel_level_mask.astype(jnp.bfloat16)
    local_pts = lax.all_to_all(localized, "mem", split_axis=2, concat_axis=0, tiled=True)
    analysis_increment = jnp.einsum(
        "mvlp,mlp->vlp", ens_perturb, local_pts, preferred_element_type=jnp.float32
    )
    analysis_increment = (analysis_increment * ens_scale).astype(jnp.bfloat16)
    gradient = observe_adjoint(analysis_increment, operator, obs_precision)
    back_pts = jnp.einsum(
        "mvlp,vlp->mlp", ens_perturb, gradient, preferred_element_type=jnp.float32
    )
    back_pts = (back_pts * ens_scale).astype(jnp.bfloat16)
    backward_values = lax.all_to_all(back_pts, "mem", split_axis=0, concat_axis=2, tiled=True)
    back_tiles = backward_values.reshape(row_total, tile_count, tile_len)
    contrib = jnp.einsum(
        "rti,tkji->rtkj", back_tiles, loc_blocks, preferred_element_type=jnp.float32
    )
    contrib = contrib.reshape(row_total, tile_count * neighbours, tile_len)
    targets = tile_index.reshape(-1)
    adjoint = jnp.zeros((row_total, tile_count, tile_len), jnp.float32).at[:, targets].add(contrib)
    return control_vec + adjoint.reshape(mem_rows, lev_rows, points)


def solution(mesh):
    return jax.shard_map(
        body,
        mesh=mesh,
        in_specs=(
            P("mem", "lev", None),
            P(None, None, "lev", "mem"),
            P(),
            P(),
            P(None, "lev", None),
            P("lev", None),
            P(None, "mem"),
        ),
        out_specs=P("mem", "lev", None),
        check_vma=False,
    )
```

profile of v0, /device:TPU:33, one launch (start us, length us, event | category | flops | bytes accessed | tf_op | source)
XLA Modules:
  0.0 473.2 jit_solution(2274181088321798920)
XLA Ops:
  6.5 0.7 compare_and_fusion
  7.2 0.7 compare_select_fusion
  7.9 0.1 copy.48
  8.1 0.1 copy.49
  8.1 0.1 reshape.61
  8.3 2.6 convert_bitcast_fusion
  10.9 0.6 copy.81
  11.5 1.4 copy.50
  12.8 15.9 %gather_fusion = bf16[576,128,128]{2,1,0:T(8,128)(2,1)} fusion(bf16[128,64,128]{2,0,1:T(8,128)(2,1)S(1)} %copy.50, s32[1024]{0:T(1024)S(1)} %pad_clamp_fusion), kind=kCustom, calls=%fused_computation | custom fusion | bytes 37751040 | tf_op jit(solution)/shard_map/jit(_take)/gather | solution.py:43
  28.8 14.5 %fusion.10 = bf16[128,64,128]{2,0,1:T(8,128)(2,1)S(1)} fusion(bf16[64,9,128,128]{3,2,1,0:T(8,128)(2,1)} %param.9, bf16[64,9,128,128]{3,2,1,0:T(8,128)(2,1)} %bitcast.64, pred[64,9]{1,0:T(8,128)(4,1)S(1)} %copy.48), kind=kOutput, calls=%fused_computation.16 | convolution fusion | flops 2426404864 | bytes 39846464 | tf_op jit(solution)/shard_map/rtkj,tkji->rti/dot_general | solution.py:44
  43.3 2.7 copy.51
  45.9 2.8 reshape.55
  48.8 13.3 %copy.52 = bf16[16,8,8192]{0,1,2:T(8,128)(2,1)} copy(bf16[16,8,8192]{2,1,0:T(8,128)(2,1)S(1)} %reshape.55) | data formatting | bytes 4194304 | tf_op jit(solution)/shard_map/reshape | solution.py:45
  62.1 20.8 %reshape.86 = bf16[16,2,32768]{2,1,0:T(2,128)(2,1)} reshape(bf16[8192,8,16]{2,1,0:T(8,128)(2,1)} %bitcast.62) | data formatting | bytes 4194304
  82.9 0.0 copy-start.2
  82.9 6.2 %all-to-all-start = ((bf16[16,2,32768]{2,1,0:T(2,128)(2,1)}), bf16[16,2,32768]{2,1,0:T(2,128)(2,1)S(1)}, u32[]{:S(2)}, u32[]{:S(2)}) async-start(bf16[16,2,32768]{2,1,0:T(2,128)(2,1)} %reshape.86), calls=%async_computation | async-start | bytes 4194304 | tf_op jit(solution)/shard_map/all_to_all | solution.py:49
  89.1 0.2 reduce-scatter.2.cloned.1.call-start
  89.3 0.0 copy-done.2
  89.4 28.4 %all-to-all-done = bf16[16,2,32768]{2,1,0:T(2,128)(2,1)S(1)} async-done(((bf16[16,2,32768]{2,1,0:T(2,128)(2,1)}), bf16[16,2,32768]{2,1,0:T(2,128)(2,1)S(1)}, u32[]{:S(2)}, u32[]{:S(2)}) %all-to-all-start) | async-done | bytes 2097184 | tf_op jit(solution)/shard_map/all_to_all | solution.py:49
  117.7 14.4 %reshape.87 = bf16[8192,8,16]{2,1,0:T(8,128)(2,1)} reshape(bf16[16,2,32768]{2,1,0:T(2,128)(2,1)S(1)} %all-to-all-done) | data formatting | bytes 4194304
  132.1 17.5 %copy.76 = bf16[16,16,8,512]{3,2,1,0:T(8,128)(2,1)S(1)} copy(bf16[16,16,8,512]{1,2,3,0:T(8,128)(2,1)} %bitcast.63) | data formatting | bytes 4194304
  149.6 0.7 bitcast_convert_fusion.1
  150.3 0.0 copy-start.1
  150.3 4.4 multiply_reduce_fusion.1
  154.7 0.0 copy-done.1
  154.7 1.1 convolution_bitcast_fusion
  155.8 0.0 reduce-scatter.2.cloned.1.call-update
  155.8 68.2 %reduce-scatter.2.cloned.1.call-done = f32[32,512]{1,0:T(8,128)} async-done(((f32[256,512]{1,0:T(8,128)}), f32[32,512]{1,0:T(8,128)}) %reduce-scatter.2.cloned.1.call-update) | async-done | bytes 65552 | tf_op jit(solution)/shard_map/reduce_scatter | solution.py:12
  224.1 0.9 multiply_convert_fusion.1
  224.9 28.1 %all_gather.3 = bf16[256,512]{1,0:T(8,128)(2,1)S(1)} all-gather(bf16[32,512]{1,0:T(8,128)(2,1)S(1)} %multiply_convert_fusion.1), channel_id=1, replica_groups=mesh['mem'=16,'lev'=8] {'lev'}, dimensions={0}, use_global_device_ids=true | all-gather | bytes 294912 | tf_op jit(solution)/shard_map/all_gather | solution.py:28
  253.1 0.1 fusion.14
  253.2 5.5 %multiply_reduce_fusion = f32[8,512,256]{1,0,2:T(8,128)S(1)} fusion(f32[8,512,3]{1,0,2:T(8,128)S(1)} %fusion.14, bf16[256,3,8,512]{3,2,1,0:T(8,128)(2,1)} %param.8), kind=kLoop, calls=%fused_computation.6 | loop fusion | flops 8388608 | bytes 10534912 | tf_op jit(solution)/shard_map/mvlp,vlp->mlp/dot_general | solution.py:55
  258.7 0.0 copy-start
  258.7 2.0 fusion.7
  260.7 14.2 %all-to-all-start.1 = ((bf16[256,8,512]{2,1,0:T(8,128)(2,1)}), bf16[256,8,512]{2,1,0:T(8,128)(2,1)S(1)}, u32[]{:S(2)}, u32[]{:S(2)}) async-start(bf16[256,8,512]{2,1,0:T(8,128)(2,1)} %fusion.7), calls=%async_computation.2 | async-start | bytes 4194304 | tf_op jit(solution)/shard_map/all_to_all | solution.py:59
  274.9 0.0 copy-done
  274.9 0.1 copy.47
  275.0 0.1 reshape.53
  275.2 28.4 %all-to-all-done.1 = bf16[256,8,512]{2,1,0:T(8,128)(2,1)S(1)} async-done(((bf16[256,8,512]{2,1,0:T(8,128)(2,1)}), bf16[256,8,512]{2,1,0:T(8,128)(2,1)S(1)}, u32[]{:S(2)}, u32[]{:S(2)}) %all-to-all-start.1) | async-done | bytes 2097184 | tf_op jit(solution)/shard_map/all_to_all | solution.py:59
  303.5 2.5 copy.55
  306.0 3.1 reshape.56
  309.1 20.8 %fusion.8 = f32[64,128,9,128]{3,1,2,0:T(8,128)} fusion(bf16[64,9,128,128]{3,2,1,0:T(8,128)(2,1)} %param.9, bf16[128,64,128,1]{2,1,0,3:T(8,128)(2,1)S(1)} %bitcast.65), kind=kOutput, calls=%fused_computation.12 | convolution fusion | flops 2415919104 | bytes 58720256 | tf_op jit(solution)/shard_map/rti,tkji->rtkj/dot_general | solution.py:61
  329.9 2.5 broadcast_in_dim.17
  332.4 116.4 %scatter_fusion = f32[128,64,128]{2,0,1:T(8,128)} fusion(f32[128,64,128]{2,0,1:T(8,128)} %broadcast_in_dim.17, s32[576]{0:T(1024)S(1)} %fusion.23, f32[576,128,128]{2,1,0:T(8,128)} %bitcast.61), kind=kCustom, calls=%fused_computation.1 | custom fusion | flops 9437184 | bytes 113248512 | tf_op jit(solution)/shard_map/scatter-add | solution.py:66
  448.9 6.5 %copy.57 = f32[128,64,128]{2,1,0:T(8,128)} copy(f32[128,64,128]{2,0,1:T(8,128)} %scatter_fusion) | data formatting | bytes 8388608 | tf_op jit(solution)/shard_map/scatter-add | solution.py:66
  455.4 4.9 %reshape.58 = f32[16,8,8192]{2,1,0:T(8,128)} reshape(f32[128,64,128]{2,1,0:T(8,128)} %copy.57) | data formatting | bytes 8388608 | tf_op jit(solution)/shard_map/reshape | solution.py:67
  460.4 6.0 %add.36 = f32[16,8,8192]{2,1,0:T(8,128)} add(f32[16,8,8192]{2,1,0:T(8,128)} %param.7, f32[16,8,8192]{2,1,0:T(8,128)} %reshape.58) | non-fusion elementwise | flops 1048576 | bytes 12582912 | tf_op jit(solution)/shard_map/add | solution.py:67
  (3 shorter events, 0.0 us)
Async XLA Ops:
  82.9 6.5 %copy-start.2 = (s32[8,256]{1,0:T(8,128)S(1)}, s32[8,256]{1,0:T(8,128)}, u32[]{:S(2)}) copy-start(s32[8,256]{1,0:T(8,128)} %param.12) | copy-start | bytes 24580
  82.9 34.9 %all-to-all-start = ((bf16[16,2,32768]{2,1,0:T(2,128)(2,1)}), bf16[16,2,32768]{2,1,0:T(2,128)(2,1)S(1)}, u32[]{:S(2)}, u32[]{:S(2)}) async-start(bf16[16,2,32768]{2,1,0:T(2,128)(2,1)} %reshape.86), calls=%async_computation | async-start | bytes 4194304 | tf_op jit(solution)/shard_map/all_to_all | solution.py:49
  89.1 134.9 %reduce-scatter.2.cloned.1.call-start = ((), (), s32[]{:S(2)}) async-start(), calls=%async_computation.3 | async-start | bytes 589824 | tf_op jit(solution)/shard_map/reduce_scatter | solution.py:12
  150.3 4.4 copy-start.1
  258.7 16.2 %copy-start = (s32[64,9]{0,1:T(8,128)S(1)}, s32[64,9]{0,1:T(8,128)}, u32[]{:S(2)}) copy-start(s32[64,9]{0,1:T(8,128)} %param.10) | copy-start | bytes 6916
  260.7 42.9 %all-to-all-start.1 = ((bf16[256,8,512]{2,1,0:T(8,128)(2,1)}), bf16[256,8,512]{2,1,0:T(8,128)(2,1)S(1)}, u32[]{:S(2)}, u32[]{:S(2)}) async-start(bf16[256,8,512]{2,1,0:T(8,128)(2,1)} %fusion.7), calls=%async_computation.2 | async-start | bytes 4194304 | tf_op jit(solution)/shard_map/all_to_all | solution.py:59
Sparse Core Ops, SparseCore 0:
  155.9 68.0 reduce-scatter.1
where the time goes:
time: 476 us; the launch traced here: 473 us
  other arithmetic  140 us (29%)
  waiting for transfers between devices  125 us (26%)
  local copies, waits for them, and re-layouts  109 us (23%)
  matrix products  36.5 us (8%)
  blocking collectives  28.1 us (6%)
  starting transfers between devices  20.7 us (4%)
  between operations  13.5 us (3%)
    scatter-add x1, other arithmetic, body(): jnp.zeros((row_total, tile_count, tile_len), jnp.float32).at[:, targets]  116 us
    reduce_scatter x1, waiting for transfers between devices, observe_adjoint(): lax.psum_scatter(jnp.einsum('bws,bwn->sn', operator_partial, analysis_inc...  68.2 us
    unnamed x11, local copies, waits for them, and re-layouts  53.3 us
    all_to_all x1, waiting for transfers between devices, body(): lax.all_to_all(localized, 'mem', split_axis=2, concat_axis=0, tiled=True)  28.4 us
    all_to_all x1, waiting for transfers between devices, body(): lax.all_to_all(back_pts, 'mem', split_axis=0, concat_axis=2, tiled=True)  28.4 us
    all_gather x1, blocking collectives, observe_adjoint(): lax.all_gather(weighted, 'lev', axis=0, tiled=True)  28.1 us
    dot_general x1, matrix products, body(): jnp.einsum('rti,tkji->rtkj', back_tiles, loc_blocks, preferred_element_ty...  20.8 us
    reshape x2, local copies, waits for them, and re-layouts, body(): localized.astype(jnp.bfloat16).reshape(mem_rows, lev_rows, points)  16.1 us
  transfers between devices with their start and end apart: 3, of which 3 were waited for; matrix products, arithmetic and copies ran while one was open for 0% of the time, Pallas kernels for 0%

commit v1 on v0

--- a/solution.py
+++ b/solution.py
@@ -25,7 +25,9 @@
     gradient = jnp.einsum(
         "nhs,sb->nhb",
         operator_partial,
-        lax.all_gather(weighted, "lev", axis=0, tiled=True),
+        jnp.concatenate(
+            lax.all_to_all(jnp.stack([weighted] * lax.axis_size("lev")), "lev", 0, 0), axis=0
+        ),
         preferred_element_type=jnp.float32,
     )
     return gradient.astype(jnp.bfloat16)

time: 476 us -> 454 us (0.954)
  blocking collectives: 28.1 us -> 11.5 us
  starting transfers between devices: 20.7 us -> 15.6 us
    all_gather x1 -> x0, blocking collectives: 28.1 us -> none  [observe_adjoint(): lax.all_gather(weighted, 'lev', axis=0, tiled=True)]
    all_to_all x0 -> x1, blocking collectives: none -> 11.5 us  [observe_adjoint(): lax.all_to_all(jnp.stack([weighted] * lax.axis_size('lev')), 'lev', 0, 0)]
    all_to_all x1, starting transfers between devices: 14.2 us -> 9.13 us  [body(): lax.all_to_all(back_pts, 'mem', split_axis=0, concat_axis=2, tiled=True)]
where the time goes in v1:
time: 454 us; the launch traced here: 451 us
  other arithmetic  140 us (31%)
  waiting for transfers between devices  125 us (28%)
  local copies, waits for them, and re-layouts  109 us (24%)
  matrix products  36.5 us (8%)
  starting transfers between devices  15.6 us (3%)
  between operations  13.5 us (3%)
  blocking collectives  11.5 us (3%)
    scatter-add x1, other arithmetic, body(): jnp.zeros((row_total, tile_count, tile_len), jnp.float32).at[:, targets]  116 us
    reduce_scatter x1, waiting for transfers between devices, observe_adjoint(): lax.psum_scatter(jnp.einsum('bws,bwn->sn', operator_partial, analysis_inc...  68.2 us
    unnamed x11, local copies, waits for them, and re-layouts  53.3 us
    all_to_all x1, waiting for transfers between devices, body(): lax.all_to_all(localized, 'mem', split_axis=2, concat_axis=0, tiled=True)  28.4 us
    all_to_all x1, waiting for transfers between devices, body(): lax.all_to_all(back_pts, 'mem', split_axis=0, concat_axis=2, tiled=True)  28.4 us
    dot_general x1, matrix products, body(): jnp.einsum('rti,tkji->rtkj', back_tiles, loc_blocks, preferred_element_ty...  20.8 us
    reshape x2, local copies, waits for them, and re-layouts, body(): localized.astype(jnp.bfloat16).reshape(mem_rows, lev_rows, points)  16.1 us
    gather x1, local copies, waits for them, and re-layouts, body(): blocks = jnp.take(control_low, tile_index, axis=1)  15.9 us
  transfers between devices with their start and end apart: 3, of which 3 were waited for; matrix products, arithmetic and copies ran while one was open for 0% of the time, Pallas kernels for 0%

profile of v1, /device:TPU:33, one launch (start us, length us, event | category | flops | bytes accessed | tf_op | source)
XLA Modules:
  0.0 451.5 jit_solution(2648715788749510991)
XLA Ops:
  6.5 0.7 compare_and_fusion
  7.2 0.7 compare_select_fusion
  7.9 0.1 copy.48
  8.1 0.1 copy.49
  8.1 0.1 reshape.67
  8.3 2.6 convert_bitcast_fusion
  10.9 0.6 copy.81
  11.5 1.4 copy.50
  12.8 15.9 %gather_fusion = bf16[576,128,128]{2,1,0:T(8,128)(2,1)} fusion(bf16[128,64,128]{2,0,1:T(8,128)(2,1)S(1)} %copy.50, s32[1024]{0:T(1024)S(1)} %pad_clamp_fusion), kind=kCustom, calls=%fused_computation | custom fusion | bytes 37751040 | tf_op jit(solution)/shard_map/jit(_take)/gather | solution.py:45
  28.8 14.5 %fusion.10 = bf16[128,64,128]{2,0,1:T(8,128)(2,1)S(1)} fusion(bf16[64,9,128,128]{3,2,1,0:T(8,128)(2,1)} %param.9, bf16[64,9,128,128]{3,2,1,0:T(8,128)(2,1)} %bitcast.65, pred[64,9]{1,0:T(8,128)(4,1)S(1)} %copy.48), kind=kOutput, calls=%fused_computation.16 | convolution fusion | flops 2426404864 | bytes 39846464 | tf_op jit(solution)/shard_map/rtkj,tkji->rti/dot_general | solution.py:46
  43.3 2.7 copy.51
  45.9 2.8 reshape.60
  48.8 13.3 %copy.52 = bf16[16,8,8192]{0,1,2:T(8,128)(2,1)} copy(bf16[16,8,8192]{2,1,0:T(8,128)(2,1)S(1)} %reshape.60) | data formatting | bytes 4194304 | tf_op jit(solution)/shard_map/reshape | solution.py:47
  62.1 20.8 %reshape.92 = bf16[16,2,32768]{2,1,0:T(2,128)(2,1)} reshape(bf16[8192,8,16]{2,1,0:T(8,128)(2,1)} %bitcast.63) | data formatting | bytes 4194304
  82.9 0.0 copy-start.2
  82.9 6.2 %all-to-all-start = ((bf16[16,2,32768]{2,1,0:T(2,128)(2,1)}), bf16[16,2,32768]{2,1,0:T(2,128)(2,1)S(1)}, u32[]{:S(2)}, u32[]{:S(2)}) async-start(bf16[16,2,32768]{2,1,0:T(2,128)(2,1)} %reshape.92), calls=%async_computation | async-start | bytes 4194304 | tf_op jit(solution)/shard_map/all_to_all | solution.py:51
  89.1 0.2 reduce-scatter.2.cloned.1.call-start
  89.3 0.0 copy-done.2
  89.4 28.4 %all-to-all-done = bf16[16,2,32768]{2,1,0:T(2,128)(2,1)S(1)} async-done(((bf16[16,2,32768]{2,1,0:T(2,128)(2,1)}), bf16[16,2,32768]{2,1,0:T(2,128)(2,1)S(1)}, u32[]{:S(2)}, u32[]{:S(2)}) %all-to-all-start) | async-done | bytes 2097184 | tf_op jit(solution)/shard_map/all_to_all | solution.py:51
  117.7 14.4 %reshape.93 = bf16[8192,8,16]{2,1,0:T(8,128)(2,1)} reshape(bf16[16,2,32768]{2,1,0:T(2,128)(2,1)S(1)} %all-to-all-done) | data formatting | bytes 4194304
  132.1 17.5 %copy.76 = bf16[16,16,8,512]{3,2,1,0:T(8,128)(2,1)S(1)} copy(bf16[16,16,8,512]{1,2,3,0:T(8,128)(2,1)} %bitcast.64) | data formatting | bytes 4194304
  149.6 0.7 bitcast_convert_fusion.1
  150.3 0.0 copy-start.1
  150.3 4.4 multiply_reduce_fusion.1
  154.7 0.0 copy-done.1
  154.7 1.1 convolution_bitcast_fusion
  155.8 0.0 reduce-scatter.2.cloned.1.call-update
  155.8 68.2 %reduce-scatter.2.cloned.1.call-done = f32[32,512]{1,0:T(8,128)} async-done(((f32[256,512]{1,0:T(8,128)}), f32[32,512]{1,0:T(8,128)}) %reduce-scatter.2.cloned.1.call-update) | async-done | bytes 65552 | tf_op jit(solution)/shard_map/reduce_scatter | solution.py:12
  224.1 0.9 multiply_convert_fusion.1
  225.0 11.5 %all_to_all.38 = bf16[8,32,512]{2,1,0:T(8,128)(2,1)S(1)} all-to-all(bf16[8,32,512]{2,1,0:T(8,128)(2,1)S(1)} %stack.2), channel_id=1, replica_groups=mesh['mem'=16,'lev'=8] {'lev'}, dimensions={0} | all-to-all | bytes 524288 | tf_op jit(solution)/shard_map/all_to_all | solution.py:29
  236.5 0.1 fusion.14
  236.6 5.5 %multiply_reduce_fusion = f32[8,512,256]{1,0,2:T(8,128)S(1)} fusion(f32[8,512,3]{1,0,2:T(8,128)S(1)} %fusion.14, bf16[256,3,8,512]{3,2,1,0:T(8,128)(2,1)} %param.8), kind=kLoop, calls=%fused_computation.6 | loop fusion | flops 8388608 | bytes 10534912 | tf_op jit(solution)/shard_map/mvlp,vlp->mlp/dot_general | solution.py:57
  242.1 0.0 copy-start
  242.1 2.0 fusion.7
  244.1 9.1 %all-to-all-start.2 = ((bf16[256,8,512]{2,1,0:T(8,128)(2,1)}), bf16[256,8,512]{2,1,0:T(8,128)(2,1)S(1)}, u32[]{:S(2)}, u32[]{:S(2)}) async-start(bf16[256,8,512]{2,1,0:T(8,128)(2,1)} %fusion.7), calls=%async_computation.3 | async-start | bytes 4194304 | tf_op jit(solution)/shard_map/all_to_all | solution.py:61
  253.2 0.0 copy-done
  253.2 0.1 copy.47
  253.3 0.1 reshape.58
  253.5 28.4 %all-to-all-done.2 = bf16[256,8,512]{2,1,0:T(8,128)(2,1)S(1)} async-done(((bf16[256,8,512]{2,1,0:T(8,128)(2,1)}), bf16[256,8,512]{2,1,0:T(8,128)(2,1)S(1)}, u32[]{:S(2)}, u32[]{:S(2)}) %all-to-all-start.2) | async-done | bytes 2097184 | tf_op jit(solution)/shard_map/all_to_all | solution.py:61
  281.8 2.5 copy.55
  284.3 3.1 reshape.62
  287.4 20.8 %fusion.8 = f32[64,128,9,128]{3,1,2,0:T(8,128)} fusion(bf16[64,9,128,128]{3,2,1,0:T(8,128)(2,1)} %param.9, bf16[128,64,128,1]{2,1,0,3:T(8,128)(2,1)S(1)} %bitcast.66), kind=kOutput, calls=%fused_computation.12 | convolution fusion | flops 2415919104 | bytes 58720256 | tf_op jit(solution)/shard_map/rti,tkji->rtkj/dot_general | solution.py:63
  308.2 2.5 broadcast_in_dim.17
  310.7 116.4 %scatter_fusion = f32[128,64,128]{2,0,1:T(8,128)} fusion(f32[128,64,128]{2,0,1:T(8,128)} %broadcast_in_dim.17, s32[576]{0:T(1024)S(1)} %fusion.22, f32[576,128,128]{2,1,0:T(8,128)} %bitcast.62), kind=kCustom, calls=%fused_computation.1 | custom fusion | flops 9437184 | bytes 113248512 | tf_op jit(solution)/shard_map/scatter-add | solution.py:68
  427.2 6.5 %copy.57 = f32[128,64,128]{2,1,0:T(8,128)} copy(f32[128,64,128]{2,0,1:T(8,128)} %scatter_fusion) | data formatting | bytes 8388608 | tf_op jit(solution)/shard_map/scatter-add | solution.py:68
  433.7 4.9 %reshape.64 = f32[16,8,8192]{2,1,0:T(8,128)} reshape(f32[128,64,128]{2,1,0:T(8,128)} %copy.57) | data formatting | bytes 8388608 | tf_op jit(solution)/shard_map/reshape | solution.py:69
  438.7 6.0 %add.36 = f32[16,8,8192]{2,1,0:T(8,128)} add(f32[16,8,8192]{2,1,0:T(8,128)} %param.7, f32[16,8,8192]{2,1,0:T(8,128)} %reshape.64) | non-fusion elementwise | flops 1048576 | bytes 12582912 | tf_op jit(solution)/shard_map/add | solution.py:69
  (4 shorter events, 0.0 us)
Async XLA Ops:
  82.9 6.5 %copy-start.2 = (s32[8,256]{1,0:T(8,128)S(1)}, s32[8,256]{1,0:T(8,128)}, u32[]{:S(2)}) copy-start(s32[8,256]{1,0:T(8,128)} %param.12) | copy-start | bytes 24580
  82.9 34.9 %all-to-all-start = ((bf16[16,2,32768]{2,1,0:T(2,128)(2,1)}), bf16[16,2,32768]{2,1,0:T(2,128)(2,1)S(1)}, u32[]{:S(2)}, u32[]{:S(2)}) async-start(bf16[16,2,32768]{2,1,0:T(2,128)(2,1)} %reshape.92), calls=%async_computation | async-start | bytes 4194304 | tf_op jit(solution)/shard_map/all_to_all | solution.py:51
  89.1 134.9 %reduce-scatter.2.cloned.1.call-start = ((), (), s32[]{:S(2)}) async-start(), calls=%async_computation.4 | async-start | bytes 589824 | tf_op jit(solution)/shard_map/reduce_scatter | solution.py:12
  150.3 4.4 copy-start.1
  242.1 11.1 %copy-start = (s32[64,9]{0,1:T(8,128)S(1)}, s32[64,9]{0,1:T(8,128)}, u32[]{:S(2)}) copy-start(s32[64,9]{0,1:T(8,128)} %param.10) | copy-start | bytes 6916
  244.1 37.8 %all-to-all-start.2 = ((bf16[256,8,512]{2,1,0:T(8,128)(2,1)}), bf16[256,8,512]{2,1,0:T(8,128)(2,1)S(1)}, u32[]{:S(2)}, u32[]{:S(2)}) async-start(bf16[256,8,512]{2,1,0:T(8,128)(2,1)} %fusion.7), calls=%async_computation.3 | async-start | bytes 4194304 | tf_op jit(solution)/shard_map/all_to_all | solution.py:61
Sparse Core Ops, SparseCore 0:
  155.9 68.0 reduce-scatter.1
